TPU v7x, 32 devices: a whole 2x2x4 slice. The times are simulated.
32 devices in a mesh: grp: 2 (over x), row: 16 (over z, y, core).
Axes of the slice: x: 2, y: 2, z: 4, core: 2. Of those that a mesh axis runs over, the one named last changes fastest.
Arguments:
- pair: bfloat16 [64, 32, 128], P(('grp', 'row')), parts along dimension 0, may hold values from -6 to 6
- chain_counts: int32 [8], P('grp'), parts along dimension 0, may hold values from 4 to 8
- w_out_proj: bfloat16 [128, 640], replicated, may hold values from -0.5 to 0.5
- w_out_final: bfloat16 [128, 128], replicated, may hold values from -0.5 to 0.5
- w_in_proj: bfloat16 [128, 640], replicated, may hold values from -0.5 to 0.5
- w_in_final: bfloat16 [128, 128], replicated, may hold values from -0.5 to 0.5
- cotangent: bfloat16 [64, 32, 128], P(('grp', 'row')), parts along dimension 0, may hold values from -6 to 6
Outputs:
- pair_out: bfloat16 [64, 32, 128], P(('grp', 'row')), parts along dimension 0
- pair_grad: bfloat16 [64, 32, 128], P(('grp', 'row')), parts along dimension 0
There are 2 independent parts, one for each index of `grp`. A program takes and returns all parts, laid end to end along the dimension named above; an argument that names none is the same for every part. Nothing has to cross between parts.
Inputs may be any that keep to these rules, and one draw needn't show every extreme that they name: `chain_counts`: tokens of a chain beyond its count, within its 8 slots, are padding.
All inputs are finite; a program needn't handle non-finite values.
Results may differ from a plain program's by a relative error of at most 0.017.
Values may be sent and summed in bfloat16 or wider, within the bound.
A program may use at most 64 MiB of HBM per device.

v0:
```python
import jax
import jax.numpy as jnp
from jax import lax
from jax.sharding import PartitionSpec as P


def token_valid(positions, counts, slot):
    chain = positions // slot
    labels = jnp.arange(counts.shape[0], dtype=jnp.int32)
    own = jnp.sum(jnp.where(chain[:, None] == labels[None, :], counts[None, :], 0), axis=1)
    return (positions % slot < own).astype(jnp.float32)


def normalize(values):
    center = values - jnp.mean(values, axis=-1, keepdims=True)
    spread = jnp.mean(center * center, axis=-1, keepdims=True)
    return center * jax.lax.rsqrt(spread + 1e-05)


def project(zfloat, mask, weight):
    hidden = weight.shape[1] // 4 - weight.shape[0] // 4
    width = zfloat.shape[-1]
    normed = normalize(zfloat).astype(jnp.bfloat16)
    lead = normed.shape[:-1]
    mixed = jnp.dot(normed.reshape(-1, width), weight, preferred_element_type=jnp.float32)
    mixed = mixed.reshape(lead + (weight.shape[1],))
    a_proj = mixed[..., :hidden]
    a_gate = mixed[..., hidden : 2 * hidden]
    b_proj = mixed[..., 2 * hidden : 3 * hidden]
    b_gate = mixed[..., 3 * hidden : 4 * hidden]
    out_gate = jax.nn.sigmoid(mixed[..., 4 * hidden :])
    left = (mask[..., None] * jax.nn.sigmoid(a_gate) * a_proj).astype(jnp.bfloat16)
    right = (mask[..., None] * jax.nn.sigmoid(b_gate) * b_proj).astype(jnp.bfloat16)
    return (left, right, out_gate)


def finish(contracted, out_gate, zfloat, final):
    normed = normalize(contracted).astype(jnp.bfloat16)
    lead = normed.shape[:-1]
    update = jnp.dot(normed.reshape(-1, final.shape[0]), final, preferred_element_type=jnp.float32)
    return zfloat + out_gate * update.reshape(lead + (final.shape[1],))


def contract(form, first, second):
    return jnp.einsum(form, first, second, preferred_element_type=jnp.float32)


def body(pair, chain_counts, w_out_proj, w_out_final, w_in_proj, w_in_final, cotangent):
    rows = pair.shape[0]
    tokens = pair.shape[1]
    slot = tokens // chain_counts.shape[0]
    positions = jnp.arange(tokens, dtype=jnp.int32)
    own_rows = lax.axis_index("row") * rows + jnp.arange(rows, dtype=jnp.int32)
    mask = (
        token_valid(own_rows, chain_counts, slot)[:, None]
        * token_valid(positions, chain_counts, slot)[None, :]
    )
    start_float = pair.astype(jnp.float32)
    left1, right1, gate1 = project(start_float, mask, w_out_proj)
    inner1 = contract("ikc,jkc->ijc", left1, lax.all_gather(right1, "row", axis=0, tiled=True))
    middle = finish(inner1, gate1, start_float, w_out_final).astype(jnp.bfloat16)
    middle_float = middle.astype(jnp.float32)
    left2, right2, gate2 = project(middle_float, mask, w_in_proj)
    left_turned, right_turned = (
        lax.all_to_all(left2, "row", split_axis=1, concat_axis=0, tiled=True),
        lax.all_to_all(right2, "row", split_axis=1, concat_axis=0, tiled=True),
    )
    inner2 = contract(
        "kic,kjc->ijc", left_turned, lax.all_gather(right_turned, "row", axis=1, tiled=True)
    )
    pair_out = finish(inner2, gate2, middle_float, w_in_final).astype(jnp.bfloat16)
    _, finish_back2 = jax.vjp(
        lambda x, g, z: finish(x, g, z, w_in_final), inner2, gate2, middle_float
    )
    d_inner2, d_gate2, d_direct1 = finish_back2(cotangent.astype(jnp.float32))
    d_inner2 = d_inner2.astype(jnp.bfloat16)
    piece = lax.all_gather(d_inner2, "row", axis=0, tiled=True)
    block = contract("kjc,ijc->kic", right2, piece)
    d_right = contract("kic,ijc->kjc", left2, piece)
    _, project_back2 = jax.vjp(lambda z: project(z, mask, w_in_proj), middle_float)
    (d_proj1,) = project_back2((block.astype(jnp.bfloat16), d_right.astype(jnp.bfloat16), d_gate2))
    grad_middle = d_direct1 + d_proj1
    _, finish_back1 = jax.vjp(
        lambda x, g, z: finish(x, g, z, w_out_final), inner1, gate1, start_float
    )
    d_inner1, d_gate1, d_direct0 = finish_back1(grad_middle)
    d_inner1 = d_inner1.astype(jnp.bfloat16)
    d_left1 = contract("ijc,jkc->ikc", d_inner1, lax.all_gather(right1, "row", axis=0, tiled=True))
    d_turned = lax.all_to_all(d_inner1, "row", split_axis=1, concat_axis=0, tiled=True)
    d_right1 = contract("ijc,ikc->jkc", d_turned, lax.all_gather(left1, "row", axis=0, tiled=True))
    _, project_back1 = jax.vjp(lambda z: project(z, mask, w_out_proj), start_float)
    (d_proj0,) = project_back1(
        (d_left1.astype(jnp.bfloat16), d_right1.astype(jnp.bfloat16), d_gate1)
    )
    pair_grad = (d_direct0 + d_proj0).astype(jnp.bfloat16)
    return (pair_out, pair_grad)


def solution(mesh):
    in_specs = (
        P(("grp", "row"), None, None),
        P("grp"),
        P(),
        P(),
        P(),
        P(),
        P(("grp", "row"), None, None),
    )
    out_specs = (P(("grp", "row"), None, None), P(("grp", "row"), None, None))
    return jax.shard_map(body, mesh=mesh, in_specs=in_specs, out_specs=out_specs, check_vma=False)
```

profile of v0, /device:TPU:0, one launch (start us, length us, event | category | flops | bytes accessed | tf_op | source)
XLA Modules:
  0.0 152.4 jit_solution(14103069373005946796)
XLA Ops:
  0.7 0.9 convert_reduce_fusion.1
  1.7 0.6 copy-done.28
  2.3 0.6 copy-done.38
  2.9 0.2 fusion.69
  3.2 1.1 fusion.2
  4.5 23.8 %all_gather.13 = bf16[32,32,128]{2,1,0:T(8,128)(2,1)S(1)} all-gather(bf16[2,32,128]{2,1,0:T(8,128)(2,1)S(1)} %get-tuple-element.23), channel_id=1, replica_groups=mesh['grp'=2,'row'=16] {'row'}, dimensions={0}, use_global_device_ids=true | all-gather | bytes 278528 | tf_op jit(solution)/shard_map/all_gather | solution.py:60
  28.3 1.4 copy.107
  29.9 0.6 fusion.75
  30.9 0.5 copy-done.32
  31.5 0.8 convert_reduce_fusion
  32.5 0.4 copy-done.7
  32.9 0.2 fusion
  33.1 0.4 copy-done.10
  33.5 0.6 copy.110
  34.1 3.6 %all-to-all-start = ((bf16[2,32,128]{2,0,1:T(2,128)(2,1)}), bf16[2,32,128]{2,0,1:T(2,128)(2,1)S(1)}, u32[]{:S(2)}, u32[]{:S(2)}) async-start(bf16[2,32,128]{2,0,1:T(2,128)(2,1)} %copy.110), calls=%async_computation | async-start | bytes 32768 | tf_op jit(solution)/shard_map/all_to_all | solution.py:66
  37.8 0.7 copy-done.15
  38.7 22.4 %all_gather.16 = bf16[32,32,128]{2,1,0:T(8,128)(2,1)S(1)} all-gather(bf16[2,32,128]{2,1,0:T(8,128)(2,1)S(1)} %get-tuple-element.22), channel_id=1, replica_groups=mesh['grp'=2,'row'=16] {'row'}, dimensions={0}, use_global_device_ids=true | all-gather | bytes 278528 | tf_op jit(solution)/shard_map/all_gather | solution.py:90
  61.1 0.6 copy.112
  61.7 0.7 copy.118
  62.4 0.7 copy.121
  63.2 1.4 copy.126
  64.6 3.5 %all-to-all-start.1 = ((bf16[2,32,128]{2,0,1:T(2,128)(2,1)}), bf16[2,32,128]{2,0,1:T(2,128)(2,1)S(1)}, u32[]{:S(2)}, u32[]{:S(2)}) async-start(bf16[2,32,128]{2,0,1:T(2,128)(2,1)} %copy.112), calls=%async_computation.1 | async-start | bytes 32768 | tf_op jit(solution)/shard_map/all_to_all | solution.py:65
  68.2 23.8 %all_gather.14 = bf16[32,32,128]{2,0,1:T(8,128)(2,1)} all-gather(bf16[32,2,128]{2,0,1:T(8,128)(2,1)S(1)} %bitcast.140), channel_id=1, replica_groups=mesh['grp'=2,'row'=16] {'row'}, dimensions={1}, use_global_device_ids=true | all-gather | bytes 278528 | tf_op jit(solution)/shard_map/all_gather | solution.py:69
  92.0 2.4 %copy.114 = bf16[32,32,128]{0,1,2:T(8,128)(2,1)S(1)} copy(bf16[32,32,128]{2,0,1:T(8,128)(2,1)} %all_gather.14) | data formatting | bytes 524288 | tf_op jit(solution)/shard_map/all_gather | solution.py:69
  94.4 0.6 copy-done.9
  95.0 0.7 copy.113
  95.8 0.7 copy.115
  96.5 2.1 %fusion.76 = f32[128,32,2]{1,2,0:T(2,128)} fusion(bf16[32,32,128]{0,1,2:T(8,128)(2,1)S(1)} %copy.114, bf16[32,2,128]{0,1,2:T(2,128)(2,1)} %copy.115), kind=kOutput, calls=%fused_computation.166 | convolution fusion | flops 524288 | bytes 311296 | tf_op jit(solution)/shard_map/kic,kjc->ijc/dot_general | solution.py:45
  98.6 1.0 copy.116
  99.7 0.2 fusion.12
  99.9 0.2 fusion.67
  100.1 0.2 copy-done.26
  100.3 0.2 copy-done.36
  100.6 19.5 %all_gather.15 = bf16[32,32,128]{2,1,0:T(8,128)(2,1)} all-gather(bf16[2,32,128]{2,1,0:T(8,128)(2,1)S(1)} %add_convert_fusion.2), channel_id=1, replica_groups=mesh['grp'=2,'row'=16] {'row'}, dimensions={0}, use_global_device_ids=true | all-gather | bytes 278528 | tf_op jit(solution)/shard_map/all_gather | solution.py:77
  120.1 2.4 %copy.117 = bf16[32,32,128]{1,0,2:T(8,128)(2,1)S(1)} copy(bf16[32,32,128]{2,1,0:T(8,128)(2,1)} %all_gather.15) | data formatting | bytes 524288 | tf_op jit(solution)/shard_map/all_gather | solution.py:77
  122.5 1.8 %fusion.77 = bf16[128,32,2]{1,2,0:T(2,128)(2,1)} fusion(bf16[32,32,128]{1,0,2:T(8,128)(2,1)S(1)} %copy.117, bf16[2,32,128]{1,0,2:T(2,128)(2,1)} %copy.118), kind=kOutput, calls=%fused_computation.167 | convolution fusion | flops 524288 | bytes 294912 | tf_op jit(solution)/shard_map/kic,ijc->kjc/dot_general | solution.py:45
  124.3 1.5 %copy.119 = bf16[128,32,2]{0,1,2:T(8,128)(2,1)} copy(bf16[128,32,2]{1,2,0:T(2,128)(2,1)} %fusion.77) | data formatting | bytes 32768 | tf_op jit(solution)/shard_map/kic,ijc->kjc/dot_general | solution.py:45
  125.9 2.1 %fusion.78 = bf16[128,32,2]{1,2,0:T(2,128)(2,1)} fusion(bf16[32,32,128]{1,0,2:T(8,128)(2,1)S(1)} %copy.117, bf16[2,32,128]{1,0,2:T(2,128)(2,1)} %copy.121), kind=kOutput, calls=%fused_computation.168 | convolution fusion | flops 524288 | bytes 294912 | tf_op jit(solution)/shard_map/kjc,ijc->kic/dot_general | solution.py:45
  128.0 1.0 copy.122
  129.0 1.6 %fusion.22 = (f32[2,32,128]{2,1,0:T(8,128)S(1)}, bf16[2,32,128]{2,1,0:T(8,128)(2,1)}, f32[2,32,128]{2,1,0:T(8,128)S(1)}, f32[2,32,128]{2,1,0:T(8,128)S(1)}, f32[...) fusion(bf16[2,32,128]{2,1,0:T(8,128)(2,1)S(1)} %copy-done.6, f32[2,32,640]{2,1,0:T(8,128)} %copy-done.2, ...), kind=kOutput, calls=%fused_computation.53 | convolution fusion | flops 2400256 | bytes 475904 | tf_op jit(solution)/shard_map/dot_general | solution.py:40
  130.7 0.2 fusion.83
  130.9 0.7 copy-done.8
  131.7 0.5 copy-done.35
  132.2 0.7 copy-done.11
  132.8 0.2 fusion.54
  133.1 0.6 copy-done.18
  133.9 0.7 copy-done.20
  134.6 0.2 fusion.13
  134.8 0.5 copy-done.33
  135.2 0.6 copy-done.31
  135.9 0.2 fusion.68
  136.3 0.6 copy.123
  136.9 3.5 %all-to-all-start.2 = ((bf16[2,32,128]{2,0,1:T(2,128)(2,1)}), bf16[2,32,128]{2,0,1:T(2,128)(2,1)S(1)}, u32[]{:S(2)}, u32[]{:S(2)}) async-start(bf16[2,32,128]{2,0,1:T(2,128)(2,1)} %copy.123), calls=%async_computation.2 | async-start | bytes 32768 | tf_op jit(solution)/shard_map/all_to_all | solution.py:89
  140.4 0.4 fusion.80
  140.9 6.0 %all-to-all-done.2 = bf16[2,32,128]{2,0,1:T(2,128)(2,1)S(1)} async-done(((bf16[2,32,128]{2,0,1:T(2,128)(2,1)}), bf16[2,32,128]{2,0,1:T(2,128)(2,1)S(1)}, u32[]{:S(2)}, u32[]{:S(2)}) %all-to-all-start.2) | async-done | bytes 16416 | tf_op jit(solution)/shard_map/all_to_all | solution.py:89
  147.0 0.4 fusion.79
  147.5 0.7 copy-done.14
  148.4 0.9 copy-done.1
  149.2 0.2 fusion.81
  149.4 0.5 copy-done.4
  150.3 0.5 copy-done.29
  150.8 0.6 copy-done.25
  151.4 0.2 fusion.56
  151.6 0.8 add_convert_fusion
  (107 shorter events, 3.1 us)
Async XLA Ops:
  0.6 32.2 %copy-start = (bf16[128,640]{1,0:T(8,128)(2,1)S(1)}, bf16[128,640]{1,0:T(8,128)(2,1)}, u32[]{:S(2)}) copy-start(bf16[128,640]{1,0:T(8,128)(2,1)} %param.11) | copy-start | bytes 491524
  0.6 0.9 copy-start.3
  1.5 1.7 %copy-start.12 = (f32[2,32]{1,0:T(2,128)}, f32[2,32]{1,0:T(2,128)S(1)}, u32[]{:S(2)}) copy-start(f32[2,32]{1,0:T(2,128)S(1)} %broadcast_multiply_fusion.4) | copy-start | bytes 772
  1.7 0.6 copy-start.28
  2.3 1.0 copy-start.24
  2.3 0.7 copy-start.38
  4.4 28.6 %copy-start.21 = (f32[2,32]{1,0:T(2,128)}, f32[2,32]{1,0:T(2,128)S(1)}, u32[]{:S(2)}) copy-start(f32[2,32]{1,0:T(2,128)S(1)} %broadcast_multiply_fusion) | copy-start | bytes 772
  30.6 0.8 copy-start.17
  30.8 0.7 copy-start.19
  30.9 0.5 copy-start.32
  31.5 0.8 copy-start.30
  32.3 0.5 copy-start.7
  32.5 0.6 copy-start.34
  32.9 0.6 copy-start.10
  33.4 5.2 %copy-start.2 = (f32[2,32,640]{2,1,0:T(8,128)}, f32[2,32,640]{2,1,0:T(8,128)S(1)}, u32[]{:S(2)}) copy-start(f32[2,32,640]{2,1,0:T(8,128)S(1)} %fusion) | copy-start | bytes 491524
  34.1 3.6 %copy-start.5 = (bf16[2,32,128]{2,1,0:T(8,128)(2,1)S(1)}, bf16[2,32,128]{2,1,0:T(8,128)(2,1)}, u32[]{:S(2)}) copy-start(bf16[2,32,128]{2,1,0:T(8,128)(2,1)} %param.13) | copy-start | bytes 49156
  34.1 30.5 %all-to-all-start = ((bf16[2,32,128]{2,0,1:T(2,128)(2,1)}), bf16[2,32,128]{2,0,1:T(2,128)(2,1)S(1)}, u32[]{:S(2)}, u32[]{:S(2)}) async-start(bf16[2,32,128]{2,0,1:T(2,128)(2,1)} %copy.110), calls=%async_computation | async-start | bytes 32768 | tf_op jit(solution)/shard_map/all_to_all | solution.py:66
  37.8 0.8 copy-start.15
  64.6 29.8 %all-to-all-start.1 = ((bf16[2,32,128]{2,0,1:T(2,128)(2,1)}), bf16[2,32,128]{2,0,1:T(2,128)(2,1)S(1)}, u32[]{:S(2)}, u32[]{:S(2)}) async-start(bf16[2,32,128]{2,0,1:T(2,128)(2,1)} %copy.112), calls=%async_computation.1 | async-start | bytes 32768 | tf_op jit(solution)/shard_map/all_to_all | solution.py:65
  94.4 0.6 copy-start.9
  99.7 0.6 copy-start.26
  99.9 0.6 copy-start.36
  128.0 1.0 copy-start.6
  128.0 1.0 copy-start.16
  128.0 1.0 copy-start.22
  128.0 1.0 copy-start.23
  128.0 1.0 copy-start.27
  128.0 1.0 copy-start.37
  130.9 0.7 copy-start.8
  131.5 0.6 copy-start.35
  132.2 0.7 copy-start.11
  133.0 0.8 copy-start.18
  133.9 0.7 copy-start.20
  134.6 0.6 copy-start.33
  135.2 0.7 copy-start.31
  136.9 10.0 %all-to-all-start.2 = ((bf16[2,32,128]{2,0,1:T(2,128)(2,1)}), bf16[2,32,128]{2,0,1:T(2,128)(2,1)S(1)}, u32[]{:S(2)}, u32[]{:S(2)}) async-start(bf16[2,32,128]{2,0,1:T(2,128)(2,1)} %copy.123), calls=%async_computation.2 | async-start | bytes 32768 | tf_op jit(solution)/shard_map/all_to_all | solution.py:89
  147.4 0.8 copy-start.14
  148.3 0.9 copy-start.1
  149.2 0.7 copy-start.4
  149.4 0.7 copy-start.13
  150.1 0.7 copy-start.29
  150.8 0.7 copy-start.25
where the time goes:
time: 154 us; the launch traced here: 152 us
  blocking collectives  89.6 us (58%)
  local copies, waits for them, and re-layouts  28.5 us (19%)
  matrix products  11.8 us (8%)
  starting transfers between devices  10.6 us (7%)
  waiting for transfers between devices  6 us (4%)
  other arithmetic  4.69 us (3%)
    all_gather x1, blocking collectives, body(): lax.all_gather(right_turned, 'row', axis=1, tiled=True)  23.8 us
    all_gather x1, blocking collectives, body(): lax.all_gather(right1, 'row', axis=0, tiled=True)  23.8 us
    all_gather x1, blocking collectives, body(): lax.all_gather(left1, 'row', axis=0, tiled=True)  22.4 us
    all_gather x1, blocking collectives, body(): piece = lax.all_gather(d_inner2, 'row', axis=0, tiled=True)  19.5 us
    unnamed x78, local copies, waits for them, and re-layouts  11.9 us
    dot_general x6, matrix products, contract(): return jnp.einsum(form, first, second, preferred_element_type=jnp.float32)  7.5 us
    all_to_all x1, waiting for transfers between devices, body(): lax.all_to_all(d_inner1, 'row', split_axis=1, concat_axis=0, tiled=True)  5.99 us
    dot_general x6, local copies, waits for them, and re-layouts, contract(): return jnp.einsum(form, first, second, preferred_element_type=jnp.float32)  3.69 us
  transfers between devices with their start and end apart: 3, of which 1 were waited for; matrix products, arithmetic and copies ran while one was open for 4% of the time, Pallas kernels for 0%

commit v1 on v0

--- a/solution.py
+++ b/solution.py
@@ -1,6 +1,10 @@
+import functools
+
 import jax
 import jax.numpy as jnp
 from jax import lax
+from jax.experimental import pallas as pl
+from jax.experimental.pallas import tpu as pltpu
 from jax.sharding import PartitionSpec as P
 
 
@@ -96,6 +100,351 @@
     return (pair_out, pair_grad)
 
 
+F32 = jnp.float32
+BF16 = jnp.bfloat16
+EPS = 1e-05
+
+
+def sigmoid(x):
+    return 0.5 * jnp.tanh(0.5 * x) + 0.5
+
+
+def matmul(x, w):
+    return jnp.dot(x.astype(BF16), w, preferred_element_type=F32)
+
+
+def matmul_t(x, w):
+    return lax.dot_general(x.astype(BF16), w, (((1,), (1,)), ((), ())), preferred_element_type=F32)
+
+
+def mean(x):
+    return jnp.mean(x, axis=-1, keepdims=True)
+
+
+def layer_norm(x):
+    center = x - mean(x)
+    scale = lax.rsqrt(mean(center * center) + EPS)
+    return center * scale, scale
+
+
+def layer_norm_back(grad, hat, scale):
+    return scale * (grad - mean(grad) - hat * mean(grad * hat))
+
+
+def rounded(x):
+    return x.astype(BF16).astype(F32)
+
+
+def gates(hidden, c):
+    part = [hidden[:, i * c : (i + 1) * c] for i in range(5)]
+    return part[0], sigmoid(part[1]), part[2], sigmoid(part[3]), sigmoid(part[4])
+
+
+def project_back(da, db, dgate, mask, saved, hat, scale, weight):
+    ap, sa, bp, sb, gate = saved
+    ma, mb = mask * da * sa, mask * db * sb
+    parts = [ma, ma * ap * (1.0 - sa), mb, mb * bp * (1.0 - sb), dgate * gate * (1.0 - gate)]
+    dhidden = jnp.concatenate([p.astype(BF16) for p in parts], axis=1)
+    return layer_norm_back(rounded(matmul_t(dhidden, weight)), hat, scale)
+
+
+def kernel(
+    n, rows, tokens, chunk, slot,
+    pair_in, counts, w1_in, v1_in, w2_in, v2_in, cot_in,
+    out_ref, grad_ref,
+    pair_all, cot_all, w1, v1, w2, v2,
+    mask, a1, b1, gate1, x, mid, a2, b2, gate2, dx, saved1, send_buf, recv_buf,
+    local_sem, own_sem, pair_send, pair_recv, cot_send, cot_recv, turn_send, turn_recv,
+):
+    me = lax.axis_index("row")
+    core = lax.rem(me, 2)
+    chip = me // 2
+    chips = n // 2
+    sibling = me + 1 - 2 * core
+    own = rows * tokens
+    c = out_ref.shape[1]
+    slotrows = 8
+
+    def device(i):
+        return {"row": i}
+
+    loads = [
+        pltpu.make_async_copy(s, d, local_sem.at[i])
+        for i, (s, d) in enumerate([(w1_in, w1), (v1_in, v1), (w2_in, w2), (v2_in, v2)])
+    ]
+    own_block = pl.ds(pl.multiple_of(me * own, own), own)
+    own_loads = [
+        pltpu.make_async_copy(pair_in, pair_all.at[own_block], own_sem.at[0]),
+        pltpu.make_async_copy(cot_in, cot_all.at[own_block], own_sem.at[1]),
+    ]
+    for copy in own_loads + loads:
+        copy.start()
+
+    barrier = pltpu.get_barrier_semaphore()
+    for t in range(1, n):
+        pl.semaphore_signal(
+            barrier, inc=1, device_id=device(lax.rem(me + t, n)),
+            device_id_type=pl.DeviceIdType.MESH,
+        )
+
+    def valid(index):
+        chain = index // slot
+        count = jnp.zeros(index.shape, jnp.int32)
+        for i in range(counts.shape[0]):
+            count = jnp.where(chain == i, counts[i], count)
+        return jnp.where(index - chain * slot < count, 1.0, 0.0)
+
+    second = valid(lax.broadcasted_iota(jnp.int32, (tokens, c), 0))
+    for i in range(tokens):
+        first = valid(jnp.full((tokens, c), i, jnp.int32))
+        mask[i * tokens : (i + 1) * tokens, :] = first * second
+
+    pl.semaphore_wait(barrier, n - 1)
+
+    def gather_sends(source, whole, send_sem, recv_sem):
+        copies = []
+        for t in range(chips):
+            target = sibling if t == 0 else lax.rem(chip + t, chips) * 2 + core
+            copies.append(
+                pltpu.make_async_remote_copy(
+                    src_ref=source, dst_ref=whole.at[own_block],
+                    send_sem=send_sem.at[t], recv_sem=recv_sem.at[me],
+                    device_id=device(target), device_id_type=pl.DeviceIdType.MESH,
+                )
+            )
+        return copies
+
+    def block_copy(whole, send_sem, recv_sem, index, send_index):
+        block = whole.at[pl.ds(pl.multiple_of(index * own, own), own)]
+        return pltpu.make_async_remote_copy(
+            src_ref=block, dst_ref=block,
+            send_sem=send_sem.at[send_index], recv_sem=recv_sem.at[index],
+            device_id=device(sibling), device_id_type=pl.DeviceIdType.MESH,
+        )
+
+    def forward(whole, send_sem, recv_sem):
+        copies = []
+        for t in range(1, chips):
+            source = lax.rem(chip + chips - t, chips) * 2 + core
+            copy = block_copy(whole, send_sem, recv_sem, source, chips - 1 + t)
+            copy.wait_recv()
+            copy.start()
+            copies.append(copy)
+        return copies
+
+    def wait_forwarded(whole, send_sem, recv_sem):
+        for t in range(chips):
+            source = lax.rem(chip + chips - t, chips) * 2 + 1 - core
+            block_copy(whole, send_sem, recv_sem, source, 0).wait_recv()
+
+    pair_copies = gather_sends(pair_in, pair_all, pair_send, pair_recv)
+    for copy in pair_copies:
+        copy.start()
+    for copy in own_loads + loads:
+        copy.wait()
+
+    z_own = pair_all[own_block, :].astype(F32)
+    hat, scale = layer_norm(z_own)
+    for i, part in enumerate(gates(matmul(hat, w1[...]), c)):
+        saved1[i] = part
+
+    pair_copies += forward(pair_all, pair_send, pair_recv)
+    cot_copies = gather_sends(cot_in, cot_all, cot_send, cot_recv)
+    for copy in cot_copies:
+        copy.start()
+    wait_forwarded(pair_all, pair_send, pair_recv)
+
+    whole_rows = tokens * tokens
+
+    def chunks(body):
+        def step(i, carry):
+            body(pl.ds(pl.multiple_of(i * chunk, chunk), chunk))
+            return carry
+
+        lax.fori_loop(0, whole_rows // chunk, step, 0)
+
+    def project1(at):
+        hat, _ = layer_norm(pair_all[at, :].astype(F32))
+        ap, sa, bp, sb, gate = gates(matmul(hat, w1[...]), c)
+        m = mask[at, :]
+        a1[at, :] = rounded(m * sa * ap)
+        b1[at, :] = rounded(m * sb * bp)
+        gate1[at, :] = gate
+
+    chunks(project1)
+    wide = 4
+
+    def product1(ib, carry):
+        base = ib * (wide * tokens)
+        sums = [jnp.zeros((tokens, c), F32) for _ in range(wide)]
+        for k in range(tokens):
+            block = b1[pl.ds(k, tokens, stride=tokens), :]
+            for u in range(wide):
+                sums[u] = sums[u] + a1[pl.ds(base + (u * tokens + k), 1), :] * block
+        for u in range(wide):
+            x[pl.ds(pl.multiple_of(base + u * tokens, tokens), tokens), :] = sums[u]
+        return carry
+
+    lax.fori_loop(0, tokens // wide, product1, 0)
+
+    cot_copies += forward(cot_all, cot_send, cot_recv)
+
+    def finish1(at):
+        y, _ = layer_norm(x[at, :])
+        middle = rounded(pair_all[at, :].astype(F32) + gate1[at, :] * matmul(y, v1[...]))
+        mid[at, :] = middle
+        hat, _ = layer_norm(middle)
+        ap, sa, bp, sb, gate = gates(matmul(hat, w2[...]), c)
+        m = mask[at, :]
+        a2[at, :] = rounded(m * sa * ap)
+        b2[at, :] = rounded(m * sb * bp)
+        gate2[at, :] = gate
+
+    chunks(finish1)
+    x1_hat, x1_scale = layer_norm(x[own_block, :])
+    update1 = matmul(x1_hat, v1[...])
+
+    def product2(ib, carry):
+        base = ib * wide
+        sums = [jnp.zeros((tokens, c), F32) for _ in range(wide)]
+        for k in range(tokens):
+            block = b2[k * tokens : (k + 1) * tokens, :]
+            for u in range(wide):
+                sums[u] = sums[u] + a2[pl.ds(base + (k * tokens + u), 1), :] * block
+        for u in range(wide):
+            x[pl.ds(pl.multiple_of((base + u) * tokens, tokens), tokens), :] = sums[u]
+        return carry
+
+    lax.fori_loop(0, tokens // wide, product2, 0)
+
+    wait_forwarded(cot_all, cot_send, cot_recv)
+
+    def back2(at):
+        hat, scale = layer_norm(x[at, :])
+        dy = rounded(matmul_t(cot_all[at, :].astype(F32) * gate2[at, :], v2[...]))
+        dx[at, :] = rounded(layer_norm_back(dy, hat, scale))
+
+    chunks(back2)
+
+    def own_rows(left, left_stride, right):
+        sums = [jnp.zeros((tokens, c), F32) for _ in range(rows)]
+        for t in range(tokens):
+            block = right(t)
+            for r in range(rows):
+                sums[r] = sums[r] + left(r, t) * block
+        return rounded(jnp.concatenate(sums, axis=0))
+
+    m_own = mask[own_block, :]
+    cot_own = cot_all[own_block, :].astype(F32)
+    mid_own = mid[own_block, :]
+    y2, _ = layer_norm(x[own_block, :])
+    update2 = matmul(y2, v2[...])
+    gate2_own = gate2[own_block, :]
+    out_ref[...] = (mid_own + gate2_own * update2).astype(BF16)
+    start = me * own
+    da2 = own_rows(
+        lambda r, t: b2[pl.ds(start + (r * tokens + t), 1), :], 0,
+        lambda t: dx[pl.ds(t, tokens, stride=tokens), :],
+    )
+    db2 = own_rows(
+        lambda r, t: a2[pl.ds(start + (r * tokens + t), 1), :], 0,
+        lambda t: dx[t * tokens : (t + 1) * tokens, :],
+    )
+    hat2, scale2 = layer_norm(mid_own)
+    saved2 = gates(matmul(hat2, w2[...]), c)
+    grad1 = cot_own + project_back(
+        da2, db2, cot_own * update2, m_own, saved2, hat2, scale2, w2[...]
+    )
+
+    dy1 = rounded(matmul_t(grad1 * saved1[4], v1[...]))
+    dx1 = rounded(layer_norm_back(dy1, x1_hat, x1_scale))
+    x[0:own, :] = dx1
+    for r in range(rows):
+        for s in range(rows):
+            send_buf[pl.ds(r * rows + s, n, stride=slotrows), :] = x[
+                pl.ds(r * tokens + s, n, stride=rows), :
+            ]
+
+    def turn_block(ref, i):
+        return ref.at[pl.ds(pl.multiple_of(i * slotrows, slotrows), slotrows)]
+
+    turns = []
+    for t in range(1, n):
+        target = lax.rem(me + t, n)
+        turns.append(
+            pltpu.make_async_remote_copy(
+                src_ref=turn_block(send_buf, target), dst_ref=turn_block(recv_buf, me),
+                send_sem=turn_send.at[t], recv_sem=turn_recv.at[t],
+                device_id=device(target), device_id_type=pl.DeviceIdType.MESH,
+            )
+        )
+    for copy in turns:
+        copy.start()
+    mine = pl.ds(pl.multiple_of(me * slotrows, slotrows), slotrows)
+    recv_buf[mine, :] = send_buf[mine, :]
+
+    da1 = own_rows(
+        lambda r, t: x[r * tokens + t : r * tokens + t + 1, :], 0,
+        lambda t: b1[t * tokens : (t + 1) * tokens, :],
+    )
+    for t in range(1, n):
+        source = lax.rem(me + n - t, n)
+        pltpu.make_async_remote_copy(
+            src_ref=turn_block(send_buf, me), dst_ref=turn_block(recv_buf, source),
+            send_sem=turn_send.at[t], recv_sem=turn_recv.at[t],
+            device_id=device(source), device_id_type=pl.DeviceIdType.MESH,
+        ).wait_recv()
+
+    def turned(r, t):
+        at = (t // rows) * slotrows + (t % rows) * rows + r
+        return recv_buf[at : at + 1, :]
+
+    db1 = own_rows(turned, 0, lambda t: a1[t * tokens : (t + 1) * tokens, :])
+    saved = [saved1[i] for i in range(5)]
+    hat1, scale1 = layer_norm(pair_all[own_block, :].astype(F32))
+    grad0 = grad1 + project_back(
+        da1, db1, grad1 * update1, m_own, saved, hat1, scale1, w1[...]
+    )
+    grad_ref[...] = grad0.astype(BF16)
+    for copy in pair_copies + cot_copies + turns:
+        copy.wait_send()
+
+
+def fused(n, pair, chain_counts, w1, v1, w2, v2, cotangent):
+    rows, tokens, c = pair.shape
+    own, whole = rows * tokens, tokens * tokens
+    any_spec = pl.BlockSpec(memory_space=pl.ANY)
+    vmem_spec = pl.BlockSpec(memory_space=pltpu.VMEM)
+    result = jax.ShapeDtypeStruct((own, c), BF16)
+    full = pltpu.VMEM((whole, c), F32)
+    chunk = min(whole, 256)
+    turn = pltpu.VMEM((n * 8, c), F32)
+    out, grad = pl.pallas_call(
+        functools.partial(kernel, n, rows, tokens, chunk, tokens // chain_counts.shape[0]),
+        out_shape=(result, result),
+        in_specs=[any_spec, pl.BlockSpec(memory_space=pltpu.SMEM)] + [any_spec] * 5,
+        out_specs=(vmem_spec, vmem_spec),
+        scratch_shapes=[pltpu.VMEM((whole, c), BF16)] * 2
+        + [pltpu.VMEM(w.shape, BF16) for w in (w1, v1, w2, v2)]
+        + [full] * 10
+        + [pltpu.VMEM((5, own, c), F32), turn, turn]
+        + [
+            pltpu.SemaphoreType.DMA((4,)),
+            pltpu.SemaphoreType.DMA((2,)),
+            pltpu.SemaphoreType.DMA((n,)),
+            pltpu.SemaphoreType.DMA((n,)),
+            pltpu.SemaphoreType.DMA((n,)),
+            pltpu.SemaphoreType.DMA((n,)),
+            pltpu.SemaphoreType.DMA((n,)),
+            pltpu.SemaphoreType.DMA((n,)),
+        ],
+        compiler_params=pltpu.CompilerParams(
+            collective_id=0, has_side_effects=True, vmem_limit_bytes=48 * 2**20
+        ),
+    )(pair.reshape(own, c), chain_counts, w1, v1, w2, v2, cotangent.reshape(own, c))
+    return out.reshape(pair.shape), grad.reshape(pair.shape)
+
+
 def solution(mesh):
     in_specs = (
         P(("grp", "row"), None, None),
@@ -107,4 +456,13 @@
         P(("grp", "row"), None, None),
     )
     out_specs = (P(("grp", "row"), None, None), P(("grp", "row"), None, None))
-    return jax.shard_map(body, mesh=mesh, in_specs=in_specs, out_specs=out_specs, check_vma=False)
+    n = mesh.shape["row"]
+
+    def run(pair, chain_counts, w1, v1, w2, v2, cotangent):
+        rows, tokens, c = pair.shape
+        small = tokens <= 32 and rows * rows <= 8 and tokens % 8 == 0 and n % 2 == 0
+        if small and (rows * tokens) % 16 == 0 and w1.shape[1] == 5 * c and c == 128:
+            return fused(n, pair, chain_counts, w1, v1, w2, v2, cotangent)
+        return body(pair, chain_counts, w1, v1, w2, v2, cotangent)
+
+    return jax.shard_map(run, mesh=mesh, in_specs=in_specs, out_specs=out_specs, check_vma=False)

time: 154 us -> 38.2 us (0.25)
  blocking collectives: 89.6 us -> 0 us
  Pallas kernels: 0 us -> 30.5 us
  local copies, waits for them, and re-layouts: 28.5 us -> 6.64 us
  matrix products: 11.8 us -> 0 us
  starting transfers between devices: 10.6 us -> 0 us
  waiting for transfers between devices: 6 us -> 0 us
  other arithmetic: 4.69 us -> 0 us
    all_gather x4 -> x0, blocking collectives: 89.6 us -> none  [the longest x1 23.8 us: body(): lax.all_gather(right_turned, 'row', axis=1, tiled=True)]
    pallas_call x0 -> x1, Pallas kernels: none -> 30.5 us  [fused(): pl.pallas_call(functools.partial(kernel, n, rows, tokens, chunk, tokens /...]
    dot_general x14 -> x0, matrix products: 11.8 us -> none  [the longest x6 7.5 us: contract(): return jnp.einsum(form, first, second, preferred_element_type=jnp.float32)]
    all_to_all x3 -> x0, starting transfers between devices: 10.6 us -> none  [the longest x1 3.63 us: body(): lax.all_to_all(right2, 'row', split_axis=1, concat_axis=0, tiled=True)]
    all_gather x4 -> x0, local copies, waits for them, and re-layouts: 7.64 us -> none  [the longest x1 2.38 us: body(): lax.all_gather(right_turned, 'row', axis=1, tiled=True)]
    all_to_all x3 -> x0, waiting for transfers between devices: 6 us -> none  [the longest x1 5.99 us: body(): lax.all_to_all(d_inner1, 'row', split_axis=1, concat_axis=0, tiled=True)]
    unnamed x78 -> x16, local copies, waits for them, and re-layouts: 11.9 us -> 6.64 us
    dot_general x6 -> x0, local copies, waits for them, and re-layouts: 3.69 us -> none  [contract(): return jnp.einsum(form, first, second, preferred_element_type=jnp.float32)]
  transfers between devices with their start and end apart: 3 -> 0, of which waited for: 1 -> 0; matrix products, arithmetic and copies ran while one was open for 4% -> 0% of each run, Pallas kernels for 0% -> 0%
where the time goes in v1:
time: 38.2 us; the launch traced here: 37.8 us
  Pallas kernels  30.5 us (80%)
  local copies, waits for them, and re-layouts  6.64 us (17%)
  between operations  0.66 us (2%)
    pallas_call x1, Pallas kernels, fused(): pl.pallas_call(functools.partial(kernel, n, rows, tokens, chunk, tokens /...  30.5 us
    unnamed x16, local copies, waits for them, and re-layouts  6.64 us

profile of v1, /device:TPU:0, one launch (start us, length us, event | category | flops | bytes accessed | tf_op | source)
XLA Modules:
  0.0 37.8 jit_solution(4752247208091970169)
XLA Ops:
  0.6 0.0 copy-start.6
  0.6 0.6 %copy-done.6 = s32[4]{0:T(128)S(1)} copy-done((s32[4]{0:T(128)S(1)}, s32[4]{0:T(128)}, u32[]{:S(2)}) %copy-start.6) | copy-done | bytes 40
  1.3 0.0 copy-start
  1.3 0.9 %copy-done = bf16[128,640]{1,0:T(8,128)(2,1)S(1)} copy-done((bf16[128,640]{1,0:T(8,128)(2,1)S(1)}, bf16[128,640]{1,0:T(8,128)(2,1)}, u32[]{:S(2)}) %copy-start) | copy-done | bytes 163864
  2.2 0.0 copy-start.1
  2.2 0.9 %copy-done.1 = bf16[128,640]{1,0:T(8,128)(2,1)S(1)} copy-done((bf16[128,640]{1,0:T(8,128)(2,1)S(1)}, bf16[128,640]{1,0:T(8,128)(2,1)}, u32[]{:S(2)}) %copy-start.1) | copy-done | bytes 163864
  3.1 0.0 copy-start.2
  3.1 0.8 %copy-done.2 = bf16[128,128]{1,0:T(8,128)(2,1)S(1)} copy-done((bf16[128,128]{1,0:T(8,128)(2,1)S(1)}, bf16[128,128]{1,0:T(8,128)(2,1)}, u32[]{:S(2)}) %copy-start.2) | copy-done | bytes 32792
  3.9 0.0 copy-start.3
  3.9 0.8 %copy-done.3 = bf16[128,128]{1,0:T(8,128)(2,1)S(1)} copy-done((bf16[128,128]{1,0:T(8,128)(2,1)S(1)}, bf16[128,128]{1,0:T(8,128)(2,1)}, u32[]{:S(2)}) %copy-start.3) | copy-done | bytes 32792
  4.6 0.0 copy-start.4
  4.6 0.7 %copy-done.4 = bf16[2,32,128]{2,1,0:T(8,128)(2,1)S(1)} copy-done((bf16[2,32,128]{2,1,0:T(8,128)(2,1)S(1)}, bf16[2,32,128]{2,1,0:T(8,128)(2,1)}, u32[]{:S(2)}) %copy-start.4) | copy-done | bytes 16408
  5.4 0.0 copy-start.5
  5.4 0.7 %copy-done.5 = bf16[2,32,128]{2,1,0:T(8,128)(2,1)S(1)} copy-done((bf16[2,32,128]{2,1,0:T(8,128)(2,1)S(1)}, bf16[2,32,128]{2,1,0:T(8,128)(2,1)}, u32[]{:S(2)}) %copy-start.5) | copy-done | bytes 16408
  6.1 30.5 %shard_map.86 = (bf16[64,128]{1,0:T(8,128)(2,1)S(1)}, bf16[64,128]{1,0:T(8,128)(2,1)S(1)}) custom-call(bf16[64,128]{1,0:T(8,128)(2,1)S(1)} %bitcast.6, s32[4]{0:T(128)S(1)} %copy-done.6, bf16[128,640]{1,0:T(8,128)(2,1)S(1)} %copy-done, bf16[128,128]{1,0:T(8,128)(2,1)S(1)} %copy-done.2, bf16[128,640]{1,0:T(8,128)(2,1)S(1)} %copy-done.1, ...), custom_call_target="tpu_custom_call" | custom-call | tf_op jit(solution)/shard_map/pallas_call | solution.py:422
  36.6 0.6 %copy.11 = bf16[2,32,128]{2,1,0:T(8,128)(2,1)} copy(bf16[2,32,128]{2,1,0:T(8,128)(2,1)S(1)} %bitcast.5) | data formatting | bytes 32768
  37.2 0.6 %copy.12 = bf16[2,32,128]{2,1,0:T(8,128)(2,1)} copy(bf16[2,32,128]{2,1,0:T(8,128)(2,1)S(1)} %bitcast.4) | data formatting | bytes 32768
Async XLA Ops:
  0.6 0.7 %copy-start.6 = (s32[4]{0:T(128)S(1)}, s32[4]{0:T(128)}, u32[]{:S(2)}) copy-start(s32[4]{0:T(128)} %counts.1) | copy-start | bytes 52
  1.3 0.9 %copy-start = (bf16[128,640]{1,0:T(8,128)(2,1)S(1)}, bf16[128,640]{1,0:T(8,128)(2,1)}, u32[]{:S(2)}) copy-start(bf16[128,640]{1,0:T(8,128)(2,1)} %w1_in.1) | copy-start | bytes 491524
  2.2 0.9 %copy-start.1 = (bf16[128,640]{1,0:T(8,128)(2,1)S(1)}, bf16[128,640]{1,0:T(8,128)(2,1)}, u32[]{:S(2)}) copy-start(bf16[128,640]{1,0:T(8,128)(2,1)} %w2_in.1) | copy-start | bytes 491524
  3.1 0.8 %copy-start.2 = (bf16[128,128]{1,0:T(8,128)(2,1)S(1)}, bf16[128,128]{1,0:T(8,128)(2,1)}, u32[]{:S(2)}) copy-start(bf16[128,128]{1,0:T(8,128)(2,1)} %v1_in.1) | copy-start | bytes 98308
  3.9 0.8 %copy-start.3 = (bf16[128,128]{1,0:T(8,128)(2,1)S(1)}, bf16[128,128]{1,0:T(8,128)(2,1)}, u32[]{:S(2)}) copy-start(bf16[128,128]{1,0:T(8,128)(2,1)} %v2_in.1) | copy-start | bytes 98308
  4.6 0.7 %copy-start.4 = (bf16[2,32,128]{2,1,0:T(8,128)(2,1)S(1)}, bf16[2,32,128]{2,1,0:T(8,128)(2,1)}, u32[]{:S(2)}) copy-start(bf16[2,32,128]{2,1,0:T(8,128)(2,1)} %param.7) | copy-start | bytes 49156
  5.4 0.7 %copy-start.5 = (bf16[2,32,128]{2,1,0:T(8,128)(2,1)S(1)}, bf16[2,32,128]{2,1,0:T(8,128)(2,1)}, u32[]{:S(2)}) copy-start(bf16[2,32,128]{2,1,0:T(8,128)(2,1)} %param.13) | copy-start | bytes 49156

commit v2 on v1

--- a/solution.py
+++ b/solution.py
@@ -121,9 +121,14 @@
     return jnp.mean(x, axis=-1, keepdims=True)
 
 
+def mean_by_matmul(x):
+    c = x.shape[1]
+    return jnp.dot(x.astype(BF16), jnp.full((c, c), 1.0 / c, BF16), preferred_element_type=F32)
+
+
 def layer_norm(x):
     center = x - mean(x)
-    scale = lax.rsqrt(mean(center * center) + EPS)
+    scale = lax.rsqrt(mean_by_matmul(center * center) + EPS)
     return center * scale, scale
 
 
@@ -150,11 +155,11 @@
 
 def kernel(
     n, rows, tokens, chunk, slot,
-    pair_in, counts, w1_in, v1_in, w2_in, v2_in, cot_in,
-    out_ref, grad_ref,
+    pair_in, counts_in, w1_in, v1_in, w2_in, v2_in, cot_in,
+    both_ref,
     pair_all, cot_all, w1, v1, w2, v2,
-    mask, a1, b1, gate1, x, mid, a2, b2, gate2, dx, saved1, send_buf, recv_buf,
-    local_sem, own_sem, pair_send, pair_recv, cot_send, cot_recv, turn_send, turn_recv,
+    counts, mask, a1, b1, gate1, x, mid, a2, b2, gate2, dx, saved1, send_buf, recv_buf,
+    counts_sem, local_sem, own_sem, pair_send, pair_recv, cot_send, cot_recv, turn_send, turn_recv,
 ):
     me = lax.axis_index("row")
     core = lax.rem(me, 2)
@@ -162,7 +167,9 @@
     chips = n // 2
     sibling = me + 1 - 2 * core
     own = rows * tokens
-    c = out_ref.shape[1]
+    c = both_ref.shape[1]
+    out_ref = both_ref.at[0:own]
+    grad_ref = both_ref.at[own : 2 * own]
     slotrows = 8
 
     def device(i):
@@ -177,7 +184,8 @@
         pltpu.make_async_copy(pair_in, pair_all.at[own_block], own_sem.at[0]),
         pltpu.make_async_copy(cot_in, cot_all.at[own_block], own_sem.at[1]),
     ]
-    for copy in own_loads + loads:
+    count_load = pltpu.make_async_copy(counts_in, counts, counts_sem)
+    for copy in [count_load] + own_loads + loads:
         copy.start()
 
     barrier = pltpu.get_barrier_semaphore()
@@ -194,6 +202,7 @@
             count = jnp.where(chain == i, counts[i], count)
         return jnp.where(index - chain * slot < count, 1.0, 0.0)
 
+    count_load.wait()
     second = valid(lax.broadcasted_iota(jnp.int32, (tokens, c), 0))
     for i in range(tokens):
         first = valid(jnp.full((tokens, c), i, jnp.int32))
@@ -257,11 +266,8 @@
     whole_rows = tokens * tokens
 
     def chunks(body):
-        def step(i, carry):
-            body(pl.ds(pl.multiple_of(i * chunk, chunk), chunk))
-            return carry
-
-        lax.fori_loop(0, whole_rows // chunk, step, 0)
+        for i in range(0, whole_rows, chunk):
+            body(pl.ds(i, chunk))
 
     def project1(at):
         hat, _ = layer_norm(pair_all[at, :].astype(F32))
@@ -272,7 +278,7 @@
         gate1[at, :] = gate
 
     chunks(project1)
-    wide = 4
+    wide = 8
 
     def product1(ib, carry):
         base = ib * (wide * tokens)
@@ -287,7 +293,6 @@
 
     lax.fori_loop(0, tokens // wide, product1, 0)
 
-    cot_copies += forward(cot_all, cot_send, cot_recv)
 
     def finish1(at):
         y, _ = layer_norm(x[at, :])
@@ -301,6 +306,7 @@
         gate2[at, :] = gate
 
     chunks(finish1)
+    cot_copies += forward(cot_all, cot_send, cot_recv)
     x1_hat, x1_scale = layer_norm(x[own_block, :])
     update1 = matmul(x1_hat, v1[...])
 
@@ -326,7 +332,7 @@
 
     chunks(back2)
 
-    def own_rows(left, left_stride, right):
+    def own_rows(left, right):
         sums = [jnp.zeros((tokens, c), F32) for _ in range(rows)]
         for t in range(tokens):
             block = right(t)
@@ -343,11 +349,11 @@
     out_ref[...] = (mid_own + gate2_own * update2).astype(BF16)
     start = me * own
     da2 = own_rows(
-        lambda r, t: b2[pl.ds(start + (r * tokens + t), 1), :], 0,
+        lambda r, t: b2[pl.ds(start + (r * tokens + t), 1), :],
         lambda t: dx[pl.ds(t, tokens, stride=tokens), :],
     )
     db2 = own_rows(
-        lambda r, t: a2[pl.ds(start + (r * tokens + t), 1), :], 0,
+        lambda r, t: a2[pl.ds(start + (r * tokens + t), 1), :],
         lambda t: dx[t * tokens : (t + 1) * tokens, :],
     )
     hat2, scale2 = layer_norm(mid_own)
@@ -384,7 +390,7 @@
     recv_buf[mine, :] = send_buf[mine, :]
 
     da1 = own_rows(
-        lambda r, t: x[r * tokens + t : r * tokens + t + 1, :], 0,
+        lambda r, t: x[r * tokens + t : r * tokens + t + 1, :],
         lambda t: b1[t * tokens : (t + 1) * tokens, :],
     )
     for t in range(1, n):
@@ -399,7 +405,7 @@
         at = (t // rows) * slotrows + (t % rows) * rows + r
         return recv_buf[at : at + 1, :]
 
-    db1 = own_rows(turned, 0, lambda t: a1[t * tokens : (t + 1) * tokens, :])
+    db1 = own_rows(turned, lambda t: a1[t * tokens : (t + 1) * tokens, :])
     saved = [saved1[i] for i in range(5)]
     hat1, scale1 = layer_norm(pair_all[own_block, :].astype(F32))
     grad0 = grad1 + project_back(
@@ -413,22 +419,24 @@
 def fused(n, pair, chain_counts, w1, v1, w2, v2, cotangent):
     rows, tokens, c = pair.shape
     own, whole = rows * tokens, tokens * tokens
-    any_spec = pl.BlockSpec(memory_space=pl.ANY)
+    hbm_spec = pl.BlockSpec(memory_space=pltpu.HBM)
     vmem_spec = pl.BlockSpec(memory_space=pltpu.VMEM)
     result = jax.ShapeDtypeStruct((own, c), BF16)
     full = pltpu.VMEM((whole, c), F32)
-    chunk = min(whole, 256)
+    chunk = whole
     turn = pltpu.VMEM((n * 8, c), F32)
-    out, grad = pl.pallas_call(
+    both = pl.pallas_call(
         functools.partial(kernel, n, rows, tokens, chunk, tokens // chain_counts.shape[0]),
-        out_shape=(result, result),
-        in_specs=[any_spec, pl.BlockSpec(memory_space=pltpu.SMEM)] + [any_spec] * 5,
-        out_specs=(vmem_spec, vmem_spec),
+        out_shape=jax.ShapeDtypeStruct((2 * own, c), BF16),
+        in_specs=[hbm_spec] * 7,
+        out_specs=vmem_spec,
         scratch_shapes=[pltpu.VMEM((whole, c), BF16)] * 2
         + [pltpu.VMEM(w.shape, BF16) for w in (w1, v1, w2, v2)]
+        + [pltpu.SMEM(chain_counts.shape, jnp.int32)]
         + [full] * 10
         + [pltpu.VMEM((5, own, c), F32), turn, turn]
         + [
+            pltpu.SemaphoreType.DMA,
             pltpu.SemaphoreType.DMA((4,)),
             pltpu.SemaphoreType.DMA((2,)),
             pltpu.SemaphoreType.DMA((n,)),
@@ -439,10 +447,11 @@
             pltpu.SemaphoreType.DMA((n,)),
         ],
         compiler_params=pltpu.CompilerParams(
-            collective_id=0, has_side_effects=True, vmem_limit_bytes=48 * 2**20
+            collective_id=0, has_side_effects=True
         ),
     )(pair.reshape(own, c), chain_counts, w1, v1, w2, v2, cotangent.reshape(own, c))
-    return out.reshape(pair.shape), grad.reshape(pair.shape)
+    both = both.reshape((2,) + pair.shape)
+    return both[0], both[1]
 
 
 def solution(mesh):

time: 38.2 us -> 27.7 us (0.73)
  local copies, waits for them, and re-layouts: 6.64 us -> 1.35 us
  Pallas kernels: 30.5 us -> 25.4 us
    unnamed x16 -> x0, local copies, waits for them, and re-layouts: 6.64 us -> none
    pallas_call x1, Pallas kernels: 30.5 us -> 25.4 us  [fused(): pl.pallas_call(functools.partial(kernel, n, rows, tokens, chunk, tokens /...]
    slice x0 -> x1, local copies, waits for them, and re-layouts: none -> 1.35 us  [fused(): return (both[0], both[1])]
where the time goes in v2:
time: 27.7 us; the launch traced here: 27.4 us
  Pallas kernels  25.4 us (92%)
  local copies, waits for them, and re-layouts  1.35 us (5%)
  between operations  0.64 us (2%)
    pallas_call x1, Pallas kernels, fused(): pl.pallas_call(functools.partial(kernel, n, rows, tokens, chunk, tokens /...  25.4 us
    slice x1, local copies, waits for them, and re-layouts, fused(): return (both[0], both[1])  1.35 us

profile of v2, /device:TPU:0, one launch (start us, length us, event | category | flops | bytes accessed | tf_op | source)
XLA Modules:
  0.0 27.4 jit_solution(8392260260642081502)
XLA Ops:
  0.6 25.4 %shard_map.86 = bf16[128,128]{1,0:T(8,128)(2,1)} custom-call(bf16[64,128]{1,0:T(8,128)(2,1)} %bitcast.4, s32[4]{0:T(128)} %counts_in.1, bf16[128,640]{1,0:T(8,128)(2,1)} %w1_in.1, bf16[128,128]{1,0:T(8,128)(2,1)} %v1_in.1, bf16[128,640]{1,0:T(8,128)(2,1)} %w2_in.1, bf16[128,128]{1,0:T(8,128)(2,1)} %v2_in.1, bf16[64,128]{1,0:T(8,128)(2,1)} %bitcast.5), custom_call_target="tpu_custom_call" | custom-call | tf_op jit(solution)/shard_map/pallas_call | solution.py:428
  26.1 1.3 %fusion = (bf16[64,128]{1,0:T(8,128)(2,1)}, bf16[64,128]{1,0:T(8,128)(2,1)}) fusion(bf16[128,128]{1,0:T(8,128)(2,1)} %shard_map.86), kind=kLoop, calls=%fused_computation | loop fusion | bytes 65536 | tf_op jit(solution)/shard_map/slice | solution.py:454

commit v3 on v2

--- a/solution.py
+++ b/solution.py
@@ -288,10 +288,11 @@
             for u in range(wide):
                 sums[u] = sums[u] + a1[pl.ds(base + (u * tokens + k), 1), :] * block
         for u in range(wide):
-            x[pl.ds(pl.multiple_of(base + u * tokens, tokens), tokens), :] = sums[u]
+            x[pl.ds(base + u * tokens, tokens), :] = sums[u]
         return carry
 
-    lax.fori_loop(0, tokens // wide, product1, 0)
+    for ib in range(tokens // wide):
+        product1(ib, 0)
 
 
     def finish1(at):
@@ -318,10 +319,11 @@
             for u in range(wide):
                 sums[u] = sums[u] + a2[pl.ds(base + (k * tokens + u), 1), :] * block
         for u in range(wide):
-            x[pl.ds(pl.multiple_of((base + u) * tokens, tokens), tokens), :] = sums[u]
+            x[pl.ds((base + u) * tokens, tokens), :] = sums[u]
         return carry
 
-    lax.fori_loop(0, tokens // wide, product2, 0)
+    for ib in range(tokens // wide):
+        product2(ib, 0)
 
     wait_forwarded(cot_all, cot_send, cot_recv)
 

time: 27.7 us -> 27.1 us (0.978)
  Pallas kernels: 25.4 us -> 24.9 us
    pallas_call x1, Pallas kernels: 25.4 us -> 24.9 us  [fused(): pl.pallas_call(functools.partial(kernel, n, rows, tokens, chunk, tokens /...]
where the time goes in v3:
time: 27.1 us; the launch traced here: 26.8 us
  Pallas kernels  24.9 us (92%)
  local copies, waits for them, and re-layouts  1.35 us (5%)
  between operations  0.64 us (2%)
    pallas_call x1, Pallas kernels, fused(): pl.pallas_call(functools.partial(kernel, n, rows, tokens, chunk, tokens /...  24.9 us
    slice x1, local copies, waits for them, and re-layouts, fused(): return (both[0], both[1])  1.35 us

profile of v3, /device:TPU:0, one launch (start us, length us, event | category | flops | bytes accessed | tf_op | source)
XLA Modules:
  0.0 26.8 jit_solution(2558666461057185505)
XLA Ops:
  0.6 24.9 %shard_map.86 = bf16[128,128]{1,0:T(8,128)(2,1)} custom-call(bf16[64,128]{1,0:T(8,128)(2,1)} %bitcast.4, s32[4]{0:T(128)} %counts_in.1, bf16[128,640]{1,0:T(8,128)(2,1)} %w1_in.1, bf16[128,128]{1,0:T(8,128)(2,1)} %v1_in.1, bf16[128,640]{1,0:T(8,128)(2,1)} %w2_in.1, bf16[128,128]{1,0:T(8,128)(2,1)} %v2_in.1, bf16[64,128]{1,0:T(8,128)(2,1)} %bitcast.5), custom_call_target="tpu_custom_call" | custom-call | tf_op jit(solution)/shard_map/pallas_call | solution.py:430
  25.5 1.3 %fusion = (bf16[64,128]{1,0:T(8,128)(2,1)}, bf16[64,128]{1,0:T(8,128)(2,1)}) fusion(bf16[128,128]{1,0:T(8,128)(2,1)} %shard_map.86), kind=kLoop, calls=%fused_computation | loop fusion | bytes 65536 | tf_op jit(solution)/shard_map/slice | solution.py:456
